TPU v7x, 128 devices: a whole 4x4x4 slice. The times are simulated.
128 devices in a mesh: frame: 16 (over x_lo, y, core), head: 8 (over z, x_hi).
Axes of the slice: x: 4 (x_hi: 2, x_lo: 2; x = x_hi * 2 + x_lo), y: 4, z: 4, core: 2. Of those that a mesh axis runs over, the one named last changes fastest.
Arguments:
- queries: bfloat16 [12288, 40, 128], P('frame', 'head')
- keys_values: bfloat16 [2, 12288, 40, 128], P(None, 'frame', 'head')
- head_kind: int32 [40], P('head'), may hold values from 0 to 1, as said below
- tile_neighbours: int32 [32, 2], P('frame'), may hold values from 0 to 31, as said below
- tile_mask: int32 [32, 2], P('frame'), may hold values 0 or 1
- out_weight: bfloat16 [5120, 5120], P('head'), may hold values from -0.078125 to 0.078125
Outputs:
- projected: bfloat16 [12288, 5120], P(('frame', 'head'))
Inputs may be any that keep to these rules, and one draw needn't show every extreme that they name: `head_kind`: each aligned block of 5 heads holds at most 2 temporal heads, and some block holds exactly 2. `tile_neighbours`: row g names 2 distinct tiles other than g, each in the partition of g (partition g // 2), among the last 1 tiles of the partition before it, or among the first 1 tiles of the partition after it.
All inputs are finite; a program needn't handle non-finite values. No bound on the sum of `tile_mask` on one device may be relied on, other than what follows from the above.
Results may differ from a plain program's by a relative error of at most 0.015.
Values may be sent and summed in bfloat16 or wider, within the bound.
A program may use at most 128 MiB of HBM per device.

v0:
```python
import jax
import jax.numpy as jnp
from jax import lax
from jax.sharding import PartitionSpec as P

FACE = 1


def extended(cells, sides, width):
    for axis, dim in sides:
        count = lax.axis_size(axis)
        ends = count - 1
        head = lax.slice_in_dim(cells, 0, width, axis=dim)
        tail = lax.slice_in_dim(cells, cells.shape[dim] - width, cells.shape[dim], axis=dim)
        cells = jnp.concatenate(
            [
                lax.ppermute(tail, axis, [(i, (i + 1) % count) for i in range(ends)]),
                cells,
                lax.ppermute(head, axis, [((i + 1) % count, i) for i in range(ends)]),
            ],
            axis=dim,
        )
    return cells


def advance(current, query_rows, key_rows, value_rows):
    running_max, running_sum, weighted = current
    score_scale = query_rows.shape[1] ** (-0.5)
    scores = (
        lax.dot_general(
            query_rows, key_rows, (((1,), (1,)), ((), ())), preferred_element_type=jnp.float32
        )
        * score_scale
    )
    newest = jnp.maximum(running_max, jnp.max(scores, axis=1))
    exponent = jnp.exp(scores - newest[:, None])
    factor = jnp.exp(running_max - newest)
    running_sum = running_sum * factor + jnp.sum(exponent, axis=1)
    weighted = weighted * factor[:, None] + jnp.dot(
        exponent.astype(jnp.bfloat16), value_rows, preferred_element_type=jnp.float32
    )
    return (newest, running_sum, weighted)


def sweep_keys(current, query_rows, key_rows, value_rows):
    length = key_rows.shape[0]
    block_rows = length
    while block_rows > 2048 and block_rows % 2 == 0:
        block_rows = block_rows // 2

    def visit(position, carried):
        offset = position * block_rows
        key_block = lax.dynamic_slice_in_dim(key_rows, offset, block_rows, 0)
        value_block = lax.dynamic_slice_in_dim(value_rows, offset, block_rows, 0)
        return advance(carried, query_rows, key_block, value_block)

    return lax.fori_loop(0, length // block_rows, visit, current)


def keep_state(current, query_rows, key_rows, value_rows):
    return current


def fold_heads(carried, shard_piece, active_flags, query_set):
    running_max, running_sum, weighted = carried
    max_list, sum_list, weighted_list = ([], [], [])
    for slot_index in range(running_max.shape[0]):
        current = (running_max[slot_index], running_sum[slot_index], weighted[slot_index])
        current = lax.cond(
            active_flags[slot_index],
            sweep_keys,
            keep_state,
            current,
            query_set[:, slot_index, :],
            shard_piece[0, :, slot_index, :],
            shard_piece[1, :, slot_index, :],
        )
        max_list.append(current[0])
        sum_list.append(current[1])
        weighted_list.append(current[2])
    return (jnp.stack(max_list), jnp.stack(sum_list), jnp.stack(weighted_list))


def start_state(slot_count, tok_rows, head_width):
    return (
        jnp.full((slot_count, tok_rows), -jnp.inf, jnp.float32),
        jnp.zeros((slot_count, tok_rows), jnp.float32),
        jnp.zeros((slot_count, tok_rows, head_width), jnp.float32),
    )


def tile_attention(query_part, window_part, key_ids, allowed_keys):
    tiles_local, tile_rows, head_width = query_part.shape
    score_scale = head_width ** (-0.5)
    gathered = window_part[:, key_ids].reshape(
        2, tiles_local, key_ids.shape[1] * tile_rows, head_width
    )
    scores = (
        jnp.einsum("tqd,tkd->tqk", query_part, gathered[0], preferred_element_type=jnp.float32)
        * score_scale
    )
    scores = jnp.where(allowed_keys[:, None, :], scores, -1e30)
    top_score = jnp.max(scores, axis=2, keepdims=True)
    exponent = jnp.where(allowed_keys[:, None, :], jnp.exp(scores - top_score), 0.0)
    weight_sum = jnp.sum(exponent, axis=2, keepdims=True)
    mixed = jnp.einsum(
        "tqk,tkd->tqd",
        exponent.astype(jnp.bfloat16),
        gathered[1],
        preferred_element_type=jnp.float32,
    )
    return (mixed / weight_sum).reshape(tiles_local * tile_rows, head_width)


def skip_tiles(query_part, window_part, key_ids, allowed_keys):
    tiles_local, tile_rows, head_width = query_part.shape
    return jnp.zeros((tiles_local * tile_rows, head_width), jnp.float32)


def per_device(queries, keys_values, head_kind, tile_neighbours, tile_mask, out_weight):
    tok_rows, heads_local, head_width = queries.shape
    tiles_local = tile_neighbours.shape[0]
    tile_rows = tok_rows // tiles_local
    is_temporal = head_kind == 1
    running_max, running_sum, weighted = fold_heads(
        start_state(heads_local, tok_rows, head_width),
        lax.all_gather(keys_values, "frame", axis=1, tiled=True),
        is_temporal,
        queries,
    )
    safe_sum = jnp.where(is_temporal[:, None], running_sum, 1.0)
    temporal_out = weighted / safe_sum[:, :, None]
    halo_kv = extended(keys_values, (("frame", 1),), FACE * tile_rows)
    window_tiles = halo_kv.reshape(2, tiles_local + 2 * FACE, tile_rows, heads_local, head_width)
    partition = lax.axis_index("frame")
    local_ids = tile_neighbours - (partition * tiles_local - FACE)
    own_ids = FACE + jnp.arange(tiles_local, dtype=jnp.int32)
    key_ids = jnp.concatenate([own_ids[:, None], local_ids], axis=1)
    allowed_tiles = jnp.concatenate(
        [jnp.ones((tiles_local, 1), dtype=bool), tile_mask == 1], axis=1
    )
    allowed_keys = jnp.repeat(allowed_tiles, tile_rows, axis=1)
    query_tiles = queries.reshape(tiles_local, tile_rows, heads_local, head_width)
    head_outputs = []
    for head_index in range(heads_local):
        sliding_out = lax.cond(
            is_temporal[head_index],
            skip_tiles,
            tile_attention,
            query_tiles[:, :, head_index, :],
            window_tiles[:, :, :, head_index, :],
            key_ids,
            allowed_keys,
        )
        chosen = jnp.where(is_temporal[head_index], temporal_out[head_index], sliding_out)
        head_outputs.append(chosen.astype(jnp.bfloat16))
    attention = jnp.stack(head_outputs)
    weight_heads = out_weight.reshape(heads_local, head_width, out_weight.shape[1])
    return lax.psum_scatter(
        jnp.einsum(
            "htd,hde->te", attention, weight_heads, preferred_element_type=jnp.float32
        ).astype(jnp.bfloat16),
        "head",
        scatter_dimension=0,
        tiled=True,
    )


def solution(mesh):
    return jax.shard_map(
        per_device,
        mesh=mesh,
        in_specs=(
            P("frame", "head", None),
            P(None, "frame", "head", None),
            P("head"),
            P("frame", None),
            P("frame", None),
            P("head", None),
        ),
        out_specs=P(("frame", "head"), None),
        check_vma=False,
    )
```

profile of v0, /device:TPU:8, one launch (start us, length us, event | category | flops | bytes accessed | tf_op | source)
XLA Modules:
  0.0 498.1 jit_solution(1592477021902747957)
XLA Ops:
  7.3 3.0 fusion.280
  12.2 3.6 collective-permute-start.1
  20.4 14.6 %collective-permute-done = bf16[2,384,5,128]{3,1,2,0:T(8,128)(2,1)S(1)} collective-permute-done((bf16[2,384,5,128]{3,1,2,0:T(8,128)(2,1)}, bf16[2,384,5,128]{3,1,2,0:T(8,128)(2,1)S(1)}, u32[]{:S(2)}, u32[]{:S(2)}) %collective-permute-start) | collective-permute-done | bytes 983072 | tf_op jit(solution)/shard_map/ppermute | solution.py:17
  35.0 7.0 %collective-permute-done.1 = bf16[2,384,5,128]{3,1,2,0:T(8,128)(2,1)} collective-permute-done((bf16[2,384,5,128]{3,1,2,0:T(8,128)(2,1)}, bf16[2,384,5,128]{3,1,2,0:T(8,128)(2,1)}, u32[]{:S(2)}, u32[]{:S(2)}) %collective-permute-start.1) | collective-permute-done | bytes 983072 | tf_op jit(solution)/shard_map/ppermute | solution.py:19
  45.5 5.1 %conditional.15 = (bf16[768,128]{1,0:T(8,128)(2,1)S(1)}) conditional(s32[]{:T(128)} %convert_element_type.93, (pred[2,3,384]{2,1,0:T(4,128)(4,1)S(1)}, bf16[2,4,384,5,128]{4,2,1,0,3:T(8,128)(2,1)S(1)}, s32[2,3]{1,0:T(2,128)S(1)}, bf16[2,384,5,128]{3,1,0,2:T(8,128)(2,1)S(1)}) %tuple.336, () %tuple.182), branch_computations={%region_30.33_spmd, %region_33.34_spmd} | conditional | flops 688525312 | bytes 11043480 | solution.py:146
  48.3 2.3 fusion.8
  52.0 6.7 %conditional.17 = (bf16[768,128]{1,0:T(8,128)(2,1)S(1)}) conditional(s32[]{:T(128)} %convert_element_type.95, (pred[2,3,384]{2,1,0:T(4,128)(4,1)S(1)}, bf16[2,4,384,5,128]{4,2,1,0,3:T(8,128)(2,1)}, s32[2,3]{1,0:T(2,128)S(1)}, bf16[2,384,5,128]{3,1,0,2:T(8,128)(2,1)S(1)}) %tuple.338, () %tuple.184), branch_computations={%region_38.41_spmd, %region_41.42_spmd} | conditional | flops 688525312 | bytes 11043480 | solution.py:146
  58.7 6.3 %conditional.18 = (bf16[768,128]{1,0:T(8,128)(2,1)S(1)}) conditional(s32[]{:T(128)} %convert_element_type.96, (pred[2,3,384]{2,1,0:T(4,128)(4,1)S(1)}, bf16[2,4,384,5,128]{4,2,1,0,3:T(8,128)(2,1)}, s32[2,3]{1,0:T(2,128)S(1)}, bf16[2,384,5,128]{3,1,0,2:T(8,128)(2,1)S(1)}) %tuple.339, () %tuple.185), branch_computations={%region_42.45_spmd, %region_45.46_spmd} | conditional | flops 688525312 | bytes 11043480 | solution.py:146
  62.7 2.3 fusion.104
  65.8 113.6 %all-gather.2.cloned.1.call-done = bf16[2,12288,5,128]{3,1,2,0:T(8,128)(2,1)} async-done(((bf16[2,768,5,128]{3,1,2,0:T(8,128)(2,1)}), bf16[2,12288,5,128]{3,1,2,0:T(8,128)(2,1)}) %all-gather.2.cloned.1.call-update) | async-done | bytes 31457296 | tf_op jit(solution)/shard_map/all_gather | solution.py:127
  180.9 87.6 %conditional.11 = (f32[1,768,128]{2,1,0:T(8,128)}, f32[1,768]{1,0:T(1,128)}) conditional(s32[]{:T(128)} %convert_element_type.94, () %tuple.177, (bf16[2,12288,5,128]{3,1,2,0:T(8,128)(2,1)}, bf16[768,5,128]{2,0,1:T(8,128)(2,1)}) %tuple.176), branch_computations={%region_6.0_spmd, %region_7.0_spmd} | conditional | flops 613715712 | bytes 47833400 | solution.py:69
  180.9 4.2 slice_bitcast_fusion.8
  186.0 81.9 %while.86 = (s32[]{:T(128)}, f32[768]{0:T(1024)S(1)}, f32[768]{0:T(1024)S(1)}, f32[768,128]{1,0:T(8,128)}, bf16[12288,128]{1,0:T(8,128)(2,1)}, /*index=5*/bf16[7...) while((s32[]{:T(128)}, f32[768]{0:T(1024)S(1)}, ...), condition=%wide.region_11.0_spmd.clone, body=%wide.region_8.0_spmd.clone.sunk | while | flops 613715712 | bytes 34851016 | solution.py:57
  186.1 3.9 multiply_reduce_fusion.13
  189.9 3.3 fusion.355
  195.4 3.9 multiply_reduce_fusion.13
  199.3 3.3 fusion.355
  203.1 2.7 fusion.357
  205.8 3.9 multiply_reduce_fusion.13
  209.7 3.3 fusion.355
  213.4 2.7 fusion.357
  216.1 3.9 multiply_reduce_fusion.13
  220.0 3.3 fusion.355
  223.8 2.7 fusion.357
  226.5 3.9 multiply_reduce_fusion.13
  230.4 3.3 fusion.355
  234.1 2.7 fusion.357
  236.9 3.9 multiply_reduce_fusion.13
  240.7 3.3 fusion.355
  244.5 2.7 fusion.357
  247.2 3.9 multiply_reduce_fusion.13
  251.1 3.3 fusion.355
  254.9 2.7 fusion.357
  257.6 3.9 multiply_reduce_fusion.13
  261.5 3.3 fusion.355
  265.2 2.7 fusion.357
  271.3 87.9 %conditional.14 = (f32[1,768,128]{2,1,0:T(8,128)}, f32[1,768]{1,0:T(1,128)}) conditional(s32[]{:T(128)} %convert_element_type.97, () %tuple.180, (bf16[2,12288,5,128]{3,1,2,0:T(8,128)(2,1)}, bf16[768,5,128]{2,0,1:T(8,128)(2,1)}) %tuple.176), branch_computations={%region_24.0_spmd, %region_25.0_spmd} | conditional | flops 613715712 | bytes 47833400 | solution.py:69
  271.5 4.2 slice_bitcast_fusion.17
  276.7 81.9 %while.89 = (s32[]{:T(128)}, f32[768]{0:T(1024)S(1)}, f32[768]{0:T(1024)S(1)}, f32[768,128]{1,0:T(8,128)}, bf16[12288,128]{1,0:T(8,128)(2,1)}, /*index=5*/bf16[7...) while((s32[]{:T(128)}, f32[768]{0:T(1024)S(1)}, ...), condition=%wide.region_29.0_spmd.clone, body=%wide.region_26.0_spmd.clone.sunk | while | flops 613715712 | bytes 34851016 | solution.py:57
  276.7 3.9 multiply_reduce_fusion.10
  280.6 3.3 fusion.337
  286.1 3.9 multiply_reduce_fusion.10
  289.9 3.3 fusion.337
  293.7 2.7 fusion.339
  296.4 3.9 multiply_reduce_fusion.10
  300.3 3.3 fusion.337
  304.0 2.7 fusion.339
  306.8 3.9 multiply_reduce_fusion.10
  310.7 3.3 fusion.337
  314.4 2.7 fusion.339
  317.1 3.9 multiply_reduce_fusion.10
  321.0 3.3 fusion.337
  324.8 2.7 fusion.339
  327.5 3.9 multiply_reduce_fusion.10
  331.4 3.3 fusion.337
  335.1 2.7 fusion.339
  337.8 3.9 multiply_reduce_fusion.10
  341.7 3.3 fusion.337
  345.5 2.7 fusion.339
  348.2 3.9 multiply_reduce_fusion.10
  352.1 3.3 fusion.337
  355.8 2.7 fusion.339
  369.4 11.0 %bitcast_convert_fusion = bf16[768,5120]{1,0:T(8,128)(2,1)} fusion(bf16[5,768,128]{2,1,0:T(8,128)(2,1)S(1)} %fusion.259, bf16[5,128,5120]{2,1,0:T(8,128)(2,1)} %bitcast.387), kind=kOutput, calls=%fused_computation.240 | convolution fusion | flops 5037096960 | bytes 15400960 | tf_op jit(solution)/shard_map/htd,hde->te/dot_general | solution.py:160
  380.5 110.6 %reduce-scatter.2.cloned.1.call-done = bf16[96,5120]{1,0:T(8,128)(2,1)} async-done(((bf16[768,5120]{1,0:T(8,128)(2,1)}), bf16[96,5120]{1,0:T(8,128)(2,1)}) %reduce-scatter.2.cloned.1.call-update) | async-done | bytes 983056 | tf_op jit(solution)/shard_map/reduce_scatter | solution.py:159
  (197 shorter events, 53.6 us)
Async XLA Ops:
  6.5 35.4 %copy-start.5 = (bf16[2,768,5,128]{3,1,2,0:T(8,128)(2,1)S(1)}, bf16[2,768,5,128]{3,1,2,0:T(8,128)(2,1)}, u32[]{:S(2)}) copy-start(bf16[2,768,5,128]{3,1,2,0:T(8,128)(2,1)} %param.37) | copy-start | bytes 5898244
  6.5 9.3 %copy-start.23 = (s32[5]{0:T(128)S(1)}, s32[5]{0:T(128)}, u32[]{:S(2)}) copy-start(s32[5]{0:T(128)} %param.38) | copy-start | bytes 64
  6.5 13.7 %copy-start.22 = (s32[2,2]{1,0:T(2,128)S(1)}, s32[2,2]{1,0:T(2,128)}, u32[]{:S(2)}) copy-start(s32[2,2]{1,0:T(2,128)} %param.40) | copy-start | bytes 52
  6.5 13.8 %copy-start.21 = (s32[2,2]{1,0:T(2,128)S(1)}, s32[2,2]{1,0:T(2,128)}, u32[]{:S(2)}) copy-start(s32[2,2]{1,0:T(2,128)} %param.39) | copy-start | bytes 52
  6.5 172.8 %all-gather.2.cloned.1.call-start = ((), (), s32[]{:S(2)}) async-start(), calls=%async_computation.1 | async-start | bytes 33423360 | tf_op jit(solution)/shard_map/all_gather | solution.py:127
  7.3 483.8 %reduce-scatter.2.cloned.1.call-start = ((), (), s32[]{:S(2)}) async-start(), calls=%async_computation.2 | async-start | bytes 8847360 | tf_op jit(solution)/shard_map/reduce_scatter | solution.py:159
  10.3 24.7 %collective-permute-start = (bf16[2,384,5,128]{3,1,2,0:T(8,128)(2,1)}, bf16[2,384,5,128]{3,1,2,0:T(8,128)(2,1)S(1)}, u32[]{:S(2)}, u32[]{:S(2)}) collective-permute-start(bf16[2,384,5,128]{3,1,2,0:T(8,128)(2,1)} %get-tuple-element.1055), channel_id=1, source_target_pairs={{0,8},{8,16},{16,24},{24,32},{32,40},{40,48},{48,56},{56,64},{64,7... | collective-permute-start | bytes 2949128 | tf_op jit(solution)/shard_map/ppermute | solution.py:17
  12.2 29.8 %collective-permute-start.1 = (bf16[2,384,5,128]{3,1,2,0:T(8,128)(2,1)}, bf16[2,384,5,128]{3,1,2,0:T(8,128)(2,1)}, u32[]{:S(2)}, u32[]{:S(2)}) collective-permute-start(bf16[2,384,5,128]{3,1,2,0:T(8,128)(2,1)} %get-tuple-element.1056), channel_id=1, source_target_pairs={{8,0},{16,8},{24,16},{32,24},{40,32},{48,40},{56,48},{64,56},{72,6... | collective-permute-start | bytes 2949128 | tf_op jit(solution)/shard_map/ppermute | solution.py:19
  15.9 0.5 copy-start.17
  43.3 1.2 copy-start.7
  43.6 1.9 copy-start.6
  50.6 0.7 copy-start.9
  51.3 0.7 copy-start.11
  65.1 0.7 copy-start.13
  65.8 113.6 %copy-start.15 = (bf16[768,128]{1,0:T(8,128)(2,1)}, bf16[768,128]{1,0:T(8,128)(2,1)S(1)}, u32[]{:S(2)}) copy-start(bf16[768,128]{1,0:T(8,128)(2,1)S(1)} %get-tuple-element.1506) | copy-start | bytes 589828
  180.3 0.6 copy-start.19
  189.9 3.8 copy-start.1
  199.3 3.8 copy-start.1
  209.7 3.8 copy-start.1
  220.0 3.8 copy-start.1
  230.4 3.8 copy-start.1
  240.7 3.8 copy-start.1
  251.1 3.8 copy-start.1
  261.5 3.8 copy-start.1
  269.3 0.6 copy-start.20
  271.3 88.7 %copy-start.18 = (pred[5]{0:T(512)(128)(4,1)S(1)}, pred[5]{0:T(512)(128)(4,1)}, u32[]{:S(2)}) copy-start(pred[5]{0:T(512)(128)(4,1)} %copy-done.17) | copy-start | bytes 19
  280.6 3.8 copy-start.4
  289.9 3.8 copy-start.4
  300.3 3.8 copy-start.4
  310.6 3.8 copy-start.4
  321.0 3.8 copy-start.4
  331.4 3.8 copy-start.4
  341.7 3.8 copy-start.4
  352.1 3.8 copy-start.4
  359.2 6.7 %copy-start.10 = (bf16[768,128]{1,0:T(8,128)(2,1)S(1)}, bf16[768,128]{1,0:T(8,128)(2,1)}, u32[]{:S(2)}) copy-start(bf16[768,128]{1,0:T(8,128)(2,1)} %copy-done.9) | copy-start | bytes 589828
  361.0 5.5 %copy-start.12 = (bf16[768,128]{1,0:T(8,128)(2,1)S(1)}, bf16[768,128]{1,0:T(8,128)(2,1)}, u32[]{:S(2)}) copy-start(bf16[768,128]{1,0:T(8,128)(2,1)} %copy-done.11) | copy-start | bytes 589828
  362.1 5.8 %copy-start.14 = (bf16[768,128]{1,0:T(8,128)(2,1)S(1)}, bf16[768,128]{1,0:T(8,128)(2,1)}, u32[]{:S(2)}) copy-start(bf16[768,128]{1,0:T(8,128)(2,1)} %copy-done.13) | copy-start | bytes 589828
  363.2 5.5 %copy-start.16 = (bf16[768,128]{1,0:T(8,128)(2,1)S(1)}, bf16[768,128]{1,0:T(8,128)(2,1)}, u32[]{:S(2)}) copy-start(bf16[768,128]{1,0:T(8,128)(2,1)} %copy-done.15) | copy-start | bytes 589828
Sparse Core Ops, SparseCore 0:
  9.0 170.2 all-gather.1
  380.6 110.3 reduce-scatter.1
where the time goes:
time: 507 us; the launch traced here: 498 us
  waiting for transfers between devices  246 us (49%)
  matrix products  127 us (25%)
  other arithmetic  58.8 us (12%)
  local copies, waits for them, and re-layouts  42.5 us (8%)
  between operations  17.1 us (3%)
  starting transfers between devices  5.62 us (1%)
    all_gather x1, waiting for transfers between devices, per_device(): lax.all_gather(keys_values, 'frame', axis=1, tiled=True)  114 us
    reduce_scatter x1, waiting for transfers between devices, per_device(): lax.psum_scatter(jnp.einsum('htd,hde->te', attention, weight_heads, prefe...  111 us
    dot_general x16, matrix products, advance(): lax.dot_general(query_rows, key_rows, (((1,), (1,)), ((), ())), preferred...  62 us
    reduce_sum x16, other arithmetic, advance(): running_sum = running_sum * factor + jnp.sum(exponent, axis=1)  53 us
    dot_general x16, matrix products, advance(): jnp.dot(exponent.astype(jnp.bfloat16), value_rows, preferred_element_type...  41.6 us
    ppermute x1, waiting for transfers between devices, extended(): lax.ppermute(tail, axis, [(i, (i + 1) % count) for i in range(ends)])  14.6 us
    dot_general x1, matrix products, per_device(): jnp.einsum('htd,hde->te', attention, weight_heads, preferred_element_type...  11 us
  transfers between devices with their start and end apart: 4, of which 4 were waited for; matrix products, arithmetic and copies ran while one was open for 5% of the time, Pallas kernels for 0%

commit v1 on v0

v1 whole, which is shorter than its diff:
```python
import functools
import math

import jax
import jax.numpy as jnp
from jax import lax
from jax.experimental import pallas as pl
from jax.experimental.pallas import tpu as pltpu
from jax.sharding import PartitionSpec as P

MESH = pl.DeviceIdType.MESH
F32 = jnp.float32
BF16 = jnp.bfloat16

ROWS = 768
TILE = 384
HD = 128
D = 5120
CH = 2
CROWS = ROWS // CH
DROWS = CROWS // 8
ZROWS = 2 * DROWS
CA = 2816
CB = D - CA
HB = CB // 2
NEG = -1e30
OFF = -2e30
SCALE = HD**-0.5 * math.log2(math.e)


def dot(a, b, ca, cb):
    return lax.dot_general(a, b, (((ca,), (cb,)), ((), ())), preferred_element_type=F32)


def scores(q, k):
    scaled = q.astype(F32) * SCALE
    high = scaled.astype(BF16)
    low = (scaled - high.astype(F32)).astype(BF16)
    return dot(jnp.concatenate([high, low], axis=1), jnp.concatenate([k, k], axis=1), 1, 1)


def fold(s, v, bias, m, acc):
    tiles = len(bias)
    rows = s.shape[0]
    new = m
    for t in range(tiles):
        part = s[:, t * TILE : (t + 1) * TILE]
        top = jnp.broadcast_to(jnp.max(part, axis=1, keepdims=True), (rows, HD))
        new = jnp.maximum(new, top + bias[t])
    pieces = []
    for t in range(tiles):
        sub = new - bias[t]
        for u in range(TILE // HD):
            at = t * TILE + u * HD
            pieces.append(jnp.exp2(s[:, at : at + HD] - sub).astype(BF16))
    o = dot(jnp.concatenate(pieces, axis=1), jnp.concatenate([v, jnp.ones_like(v)], axis=1), 1, 0)
    if acc is None:
        return new, o
    f = jnp.exp2(m - new)
    return new, acc * jnp.concatenate([f, f], axis=1) + o


def kernel(
    kind_ref, near_ref, mask_ref, q_ref, kv_ref, w_hbm, out_ref,
    w_ref, qall, qslide, kbuf, wbuf, tsend, trecv, tab, m_ref, acc_ref,
    osend, lsend, orecv, lrecv, attn, pbuf,
    fa, ra, xa, xb, fb, rb,
    w_sem, q_ss, q_rs, t_ss, t_rs, kx_ss, kx_rs, kc_ss, kc_rs, h_ss, h_rs,
    o_ss, o_rs, l_ss, l_rs, r_ss, r_rs,
):
    frame = lax.axis_index("frame")
    head = lax.axis_index("head")
    xl, y, c = frame // 8, (frame // 2) % 4, frame % 2
    z, xh = head // 2, head % 2

    def frame_of(a, b, d):
        return (a * 4 + b) * 2 + d

    def at_y(g):
        return (frame_of(xl, (y + g) % 4, c), head)

    core = (frame_of(xl, y, 1 - c), head)
    across = (frame_of(1 - xl, y, c), head)
    after = ((frame + 1) % 16, head)
    before = ((frame + 15) % 16, head)
    z_up = (frame, ((z + 1) % 4) * 2 + xh)
    z_down = (frame, ((z + 3) % 4) * 2 + xh)
    x_other = (frame, z * 2 + 1 - xh)

    load_w = pltpu.make_async_copy(w_hbm, w_ref, w_sem)
    load_w.start()

    barrier = pltpu.get_barrier_semaphore()
    peers = [at_y(1), at_y(2), at_y(3), core, across, after, before, z_up, z_down, x_other]
    for peer in peers:
        pl.semaphore_signal(barrier, inc=1, device_id=peer, device_id_type=MESH)
    pl.semaphore_wait(barrier, len(peers))

    def remote(src, dst, ss, rs, peer):
        return pltpu.make_async_remote_copy(
            src_ref=src, dst_ref=dst, send_sem=ss, recv_sem=rs, device_id=peer, device_id_type=MESH
        )

    sent = []

    def start(copy):
        copy.start()
        sent.append(copy)
        return copy

    kinds = [kind_ref[i] for i in range(5)]
    many = functools.reduce(jnp.add, kinds)
    order = [0] * 5
    seen = 0
    for i in range(5):
        slot = jnp.where(kinds[i] == 1, seen, many + i - seen)
        seen = seen + kinds[i]
        order = [jnp.where(slot == s, i, order[s]) for s in range(5)]
    heads_of = [range(5), range(5), range(0, 3), range(1, 4), range(2, 5)]

    def choose(s, get):
        value = get(heads_of[s][0])
        for i in heads_of[s][1:]:
            value = lax.select(order[s] == i, get(i), value)
        return value

    @pl.loop(0, ROWS // 96)
    def _(r):
        rows = pl.ds(pl.multiple_of(r * 96, 96), 96)
        for s in range(2):
            for t in range(2):
                kbuf[0, s, t, rows, :] = choose(s, lambda i: kv_ref[t, i, rows, :])

    kx = [
        start(remote(kbuf.at[0, s, :, pl.ds(0, ROWS)], kbuf.at[1, s, :, pl.ds(0, ROWS)],
                     kx_ss.at[s], kx_rs.at[s], across))
        for s in range(2)
    ]
    kc = [
        [remote(kbuf.at[b, s, :, pl.ds(0, ROWS)], kbuf.at[b, s, :, pl.ds(ROWS, ROWS)],
                kc_ss.at[b, s], kc_rs.at[b, s], core) for s in range(2)]
        for b in range(2)
    ]
    for s in range(2):
        start(kc[0][s])
    def stage_queries(slots, store):
        for k in range(CH):

            @pl.loop(0, 8)
            def _(d):
                dest = ((z + d // 2) % 4) * 2 + (xh + d % 2) % 2
                rows = pl.ds(pl.multiple_of((dest * CH + k) * DROWS, 16), DROWS)
                to = pl.ds(pl.multiple_of(k * CROWS + d * DROWS, 16), DROWS)
                for s in slots:
                    store(s, to, choose(s, lambda i: q_ref[i, rows, :]))

    def store_temporal(s, to, value):
        qall[0, s, to, :] = value

    def store_sliding(s, to, value):
        qslide[s - 2, to, :] = value

    stage_queries(range(2), store_temporal)

    def allowed(half, ids):
        hit = ids == frame * 2 + half
        for n in range(2):
            listed = jnp.where(mask_ref[half, n] == 1, near_ref[half, n], -5)
            hit = hit | (ids == listed)
        return hit

    lane_ids = lax.broadcasted_iota(jnp.int32, (1, HD), 1)
    for s in range(2):
        shift = jnp.where(s < many, 0.0, OFF)
        for half in range(2):
            tsend[s * 2 + half : s * 2 + half + 1, :] = jnp.where(allowed(half, lane_ids), 0.0, shift)
    tsend[4:8, :] = jnp.zeros((4, HD), F32)
    window_ids = frame * 2 - 1 + lax.broadcasted_iota(jnp.int32, (8, HD), 0)
    window = [jnp.where(allowed(half, window_ids), 0.0, OFF) for half in range(2)]
    qx, tx = [None] * 4, [None] * 4
    for g in (1, 3, 2):
        tx[g] = start(remote(tsend, trecv.at[4 - g], t_ss.at[g], t_rs.at[4 - g], at_y(g)))
        qx[g] = start(remote(qall.at[0], qall.at[4 - g], q_ss.at[g], q_rs.at[4 - g], at_y(g)))

    @pl.loop(0, ROWS // 96)
    def _(r):
        rows = pl.ds(pl.multiple_of(r * 96, 96), 96)
        to = pl.ds(pl.multiple_of(TILE + r * 96, 96), 96)
        for s in range(3):
            for t in range(2):
                wbuf[s, t, to, :] = choose(s + 2, lambda i: kv_ref[t, i, rows, :])

    h_next = start(remote(wbuf.at[:, :, pl.ds(2 * TILE, TILE)], wbuf.at[:, :, pl.ds(0, TILE)],
                          h_ss.at[0], h_rs.at[0], after))
    h_prev = start(remote(wbuf.at[:, :, pl.ds(TILE, TILE)], wbuf.at[:, :, pl.ds(3 * TILE, TILE)],
                          h_ss.at[1], h_rs.at[1], before))

    def spread(src, g):
        for i in range(4):
            row = jnp.broadcast_to(src[i : i + 1, :], (128, 128))
            tab[g, i] = jnp.transpose(row)[0:32]

    spread(tsend[...], 0)
    stage_queries(range(2, 5), store_sliding)

    half_of = [((z + zr) % 4) // 2 for zr in range(4)]

    def rows_bias(get):
        low, high = get(0), get(1)
        blocks = []
        for zr in range(4):
            pick = jnp.where(half_of[zr] == 0, low, high)
            blocks.append(jnp.broadcast_to(pick, (ZROWS, HD)))
        return jnp.concatenate(blocks, axis=0)

    def temporal_bias(g, s, b):
        bias = []
        for d in range(2):
            part = frame_of(xl if b == 0 else 1 - xl, y, c if d == 0 else 1 - c)
            for t in range(2):
                bias.append(rows_bias(lambda half: tab[g, s * 2 + half, pl.ds(part * 2 + t, 1), :]))
        return bias

    def temporal(g, b, chunks, first):
        items = [(s, k) for s in range(2) for k in chunks]
        bias = [temporal_bias(g, s, b) for s in range(2)]

        def score(item):
            s, k = item
            return scores(qall[g, s, pl.ds(k * CROWS, CROWS), :], kbuf[b, s, 0])

        ahead = score(items[0])
        for i, (s, k) in enumerate(items):
            now = ahead
            if i + 1 < len(items):
                ahead = score(items[i + 1])
            rows = pl.ds(k * CROWS, CROWS)
            if first:
                m, acc = jnp.full((CROWS, HD), NEG, F32), None
            else:
                m, acc = m_ref[g, s, rows, :], acc_ref[g, s, rows, :]
            m, acc = fold(now, kbuf[b, s, 1], bias[s], m, acc)
            m_ref[g, s, rows, :] = m
            acc_ref[g, s, rows, :] = acc

    def send_o(g):
        for s in range(2):
            total = acc_ref[g, s, :, HD:]
            safe = jnp.where(total > 0, total, 1.0)
            osend[g, s] = (acc_ref[g, s, :, :HD] / safe).astype(BF16)
            log = m_ref[g, s] + jnp.log2(safe)
            lsend[g, s] = jnp.transpose(log)[0:8]

    def o_copies(g):
        return (
            remote(osend.at[g], orecv.at[4 - g], o_ss.at[g], o_rs.at[4 - g], at_y(g)),
            remote(lsend.at[g], lrecv.at[4 - g], l_ss.at[g], l_rs.at[4 - g], at_y(g)),
        )

    for s in range(2):
        kc[0][s].wait_recv()
    temporal(0, 0, range(CH), True)

    h_next.wait_recv()
    h_prev.wait_recv()

    window_bias = [
        rows_bias(lambda half, t=t: window[half][t : t + 1, :]) for t in range(4)
    ]
    items = [(s, k) for s in range(3) for k in range(CH)]
    ahead = scores(qslide[0, 0:CROWS, :], wbuf[0, 0])
    for i, (s, k) in enumerate(items):
        now = ahead
        if i + 1 < len(items):
            s1, k1 = items[i + 1]
            ahead = scores(qslide[s1, k1 * CROWS : (k1 + 1) * CROWS, :], wbuf[s1, 0])
        _, acc = fold(now, wbuf[s, 1], window_bias, jnp.full((CROWS, HD), NEG, F32), None)
        attn[k, :, (s + 2) * HD : (s + 3) * HD] = (acc[:, :HD] / acc[:, HD:]).astype(BF16)

    for g in (1, 3):
        tx[4 - g].wait_recv()
        qx[4 - g].wait_recv()
        spread(trecv[g], g)

    kx[0].wait_recv()
    start(kc[1][0])

    @pl.loop(0, 2)
    def _(i):
        temporal(1 + 2 * i, 0, range(CH), True)

    kx[1].wait_recv()
    start(kc[1][1])
    for s in range(2):
        kc[1][s].wait_recv()

    @pl.loop(0, 2)
    def _(i):
        g = 1 + 2 * i
        temporal(g, 1, range(CH), False)
        send_o(g)
        for copy in o_copies(g):
            copy.start()

    tx[2].wait_recv()
    qx[2].wait_recv()
    spread(trecv[2], 2)
    temporal(2, 0, range(CH), True)
    temporal(2, 1, range(CH), False)
    send_o(2)
    for copy in o_copies(2):
        copy.start()

    def combine(k):
        rows = pl.ds(k * CROWS, CROWS)
        for s in range(2):
            total = acc_ref[0, s, rows, HD:]
            logs = [m_ref[0, s, rows, :] + jnp.log2(total)]
            outs = [acc_ref[0, s, rows, :HD] / total]
            for g in range(1, 4):
                line = lrecv[g, s, 0:1, k * CROWS : (k + 1) * CROWS]
                logs.append(jnp.transpose(jnp.broadcast_to(line, (HD, CROWS))))
                outs.append(orecv[g, s, rows, :].astype(F32))
            top = functools.reduce(jnp.maximum, logs)
            weights = [jnp.exp2(log - top) for log in logs]
            mixed = functools.reduce(jnp.add, [w * o for w, o in zip(weights, outs)])
            attn[k, :, s * HD : (s + 1) * HD] = (
                mixed / functools.reduce(jnp.add, weights)
            ).astype(BF16)

    WIDTH = 512

    def project(k):
        slots = [attn[k, :, s * HD : (s + 1) * HD] for s in range(5)]
        for i in range(5):
            value = slots[0]
            for s in range(1, 5):
                if i in heads_of[s]:
                    value = lax.select(order[s] == i, slots[s], value)
            attn[k, :, i * HD : (i + 1) * HD] = value

        @pl.loop(0, D // WIDTH)
        def _(j):
            columns = pl.ds(pl.multiple_of(j * WIDTH, WIDTH), WIDTH)
            pbuf[k, :, columns] = dot(attn[k], w_ref[:, columns], 1, 0).astype(BF16)

    def block(k, zr, xr, first, width):
        return pbuf.at[k, pl.ds((zr * 2 + xr) * DROWS, DROWS), pl.ds(first, width)]

    def add(k, zr, xr, first, width, *others):
        @pl.loop(0, DROWS // 16)
        def _(i):
            rows = pl.ds(pl.multiple_of((zr * 2 + xr) * DROWS + i * 16, 16), 16)
            value = pbuf[k, rows, first : first + width].astype(F32)
            for other in others:
                value += other[pl.ds(pl.multiple_of(i * 16, 16), 16), :].astype(F32)
            pbuf[k, rows, first : first + width] = value.astype(BF16)

    def emit(k, first, width, *others):
        @pl.loop(0, DROWS // 16)
        def _(i):
            value = pbuf[k, pl.ds(pl.multiple_of(i * 16, 16), 16), first : first + width].astype(F32)
            for other in others:
                value += other[pl.ds(pl.multiple_of(i * 16, 16), 16), :].astype(F32)
            rows = pl.ds(pl.multiple_of(k * DROWS + i * 16, 16), 16)
            out_ref[rows, first : first + width] = value.astype(BF16)

    H1, H2 = CA, CA + HB

    class Chunk:
        def __init__(self, k):
            self.k = k
            self.count = 0

        def send(self, src, dst, peer):
            n = self.count
            self.count += 1
            return start(remote(src, dst, r_ss.at[self.k, n], r_rs.at[self.k, n], peer))

        def first(self):
            k = self.k
            self.fa = [
                self.send(block(k, 2, 0, 0, CA), fa.at[k, 0], z_up),
                self.send(block(k, 2, 1, 0, CA), fa.at[k, 1], z_down),
            ]
            self.xb = {}
            for zr in (2, 1, 3, 0):
                self.xb[zr] = self.send(block(k, zr, 1, CA, CB), xb.at[k, zr], x_other)
            self.ra = [
                self.send(block(k, 1, 1, 0, CA), ra.at[k, 0, 1], z_up),
                self.send(block(k, 3, 0, 0, CA), ra.at[k, 1, 0], z_down),
            ]

        def forward_a(self):
            k = self.k
            self.fa[0].wait_recv()
            add(k, 1, 0, 0, CA, fa.at[k, 0])
            self.ra.append(self.send(block(k, 1, 0, 0, CA), ra.at[k, 0, 0], z_up))
            self.fa[1].wait_recv()
            add(k, 3, 1, 0, CA, fa.at[k, 1])
            self.ra.append(self.send(block(k, 3, 1, 0, CA), ra.at[k, 1, 1], z_down))

        def second_b(self):
            k = self.k
            self.xb[2].wait_recv()
            add(k, 2, 0, CA, CB, xb.at[k, 2])
            self.fb = [
                self.send(block(k, 2, 0, H1, HB), fb.at[k, 0], z_up),
                self.send(block(k, 2, 0, H2, HB), fb.at[k, 1], z_down),
            ]
            self.xb[1].wait_recv()
            add(k, 1, 0, CA, CB, xb.at[k, 1])
            self.rb = [self.send(block(k, 1, 0, H2, HB), rb.at[k, 0, 1], z_up)]
            self.xb[3].wait_recv()
            add(k, 3, 0, CA, CB, xb.at[k, 3])
            self.rb.append(self.send(block(k, 3, 0, H1, HB), rb.at[k, 1, 0], z_down))

        def third_a(self):
            k = self.k
            for copy in self.ra:
                copy.wait_recv()
            add(k, 0, 1, 0, CA, ra.at[k, 0, 1], ra.at[k, 1, 1])
            self.xa = self.send(block(k, 0, 1, 0, CA), xa.at[k], x_other)

        def forward_b(self):
            k = self.k
            self.fb[0].wait_recv()
            add(k, 1, 0, H1, HB, fb.at[k, 0])
            self.rb.append(self.send(block(k, 1, 0, H1, HB), rb.at[k, 0, 0], z_up))
            self.fb[1].wait_recv()
            add(k, 3, 0, H2, HB, fb.at[k, 1])
            self.rb.append(self.send(block(k, 3, 0, H2, HB), rb.at[k, 1, 1], z_down))

        def finish(self):
            k = self.k
            self.xa.wait_recv()
            emit(k, 0, CA, ra.at[k, 0, 0], ra.at[k, 1, 0], xa.at[k])
            self.xb[0].wait_recv()
            for copy in self.rb:
                copy.wait_recv()
            emit(k, H1, HB, xb.at[k, 0, :, pl.ds(0, HB)], rb.at[k, 0, 0], rb.at[k, 1, 0])
            emit(k, H2, HB, xb.at[k, 0, :, pl.ds(HB, HB)], rb.at[k, 0, 1], rb.at[k, 1, 1])

    one, two = Chunk(0), Chunk(1)
    temporal(0, 1, [0], False)
    for g in (1, 3, 2):
        for copy in o_copies(4 - g):
            copy.wait_recv()
    combine(0)
    load_w.wait()
    project(0)
    one.first()
    temporal(0, 1, [1], False)
    combine(1)
    one.forward_a()
    project(1)
    two.first()
    one.second_b()
    two.forward_a()
    one.third_a()
    one.forward_b()
    two.second_b()
    two.third_a()
    two.forward_b()
    one.finish()
    two.finish()

    for copy in sent:
        copy.wait_send()
    for g in range(1, 4):
        for copy in o_copies(g):
            copy.wait_send()


def per_device(queries, keys_values, head_kind, tile_neighbours, tile_mask, out_weight):
    smem = pl.BlockSpec(memory_space=pltpu.SMEM)
    vmem = pl.BlockSpec(memory_space=pltpu.VMEM)
    dma = pltpu.SemaphoreType.DMA
    return pl.pallas_call(
        kernel,
        out_shape=jax.ShapeDtypeStruct((ROWS // 8, D), BF16),
        in_specs=[
            smem, smem, smem,
            vmem, vmem,
            pl.BlockSpec(memory_space=pl.ANY),
        ],
        out_specs=vmem,
        scratch_shapes=[
            pltpu.VMEM((5 * HD, D), BF16),
            pltpu.VMEM((4, 2, ROWS, HD), BF16),
            pltpu.VMEM((3, ROWS, HD), BF16),
            pltpu.VMEM((2, 2, 2, 2 * ROWS, HD), BF16),
            pltpu.VMEM((3, 2, 4 * TILE, HD), BF16),
            pltpu.VMEM((8, HD), F32),
            pltpu.VMEM((4, 8, HD), F32),
            pltpu.VMEM((4, 4, 32, HD), F32),
            pltpu.VMEM((4, 2, ROWS, HD), F32),
            pltpu.VMEM((4, 2, ROWS, 2 * HD), F32),
            pltpu.VMEM((4, 2, ROWS, HD), BF16),
            pltpu.VMEM((4, 2, 8, ROWS), F32),
            pltpu.VMEM((4, 2, ROWS, HD), BF16),
            pltpu.VMEM((4, 2, 8, ROWS), F32),
            pltpu.VMEM((CH, CROWS, 5 * HD), BF16),
            pltpu.VMEM((CH, CROWS, D), BF16),
            pltpu.VMEM((CH, 2, DROWS, CA), BF16),
            pltpu.VMEM((CH, 2, 2, DROWS, CA), BF16),
            pltpu.VMEM((CH, DROWS, CA), BF16),
            pltpu.VMEM((CH, 4, DROWS, CB), BF16),
            pltpu.VMEM((CH, 2, DROWS, HB), BF16),
            pltpu.VMEM((CH, 2, 2, DROWS, HB), BF16),
            dma,
            dma((4,)), dma((4,)),
            dma((4,)), dma((4,)),
            dma((2,)), dma((2,)),
            dma((2, 2)), dma((2, 2)),
            dma((2,)), dma((2,)),
            dma((4,)), dma((4,)),
            dma((4,)), dma((4,)),
            dma((CH, 20)), dma((CH, 20)),
        ],
        name="attend_project",
        compiler_params=pltpu.CompilerParams(
            collective_id=0, has_side_effects=True, vmem_limit_bytes=60 * 2**20
        ),
    )(
        head_kind,
        tile_neighbours,
        tile_mask,
        jnp.transpose(queries, (1, 0, 2)),
        jnp.transpose(keys_values, (0, 2, 1, 3)),
        out_weight,
    )


def solution(mesh):
    return jax.shard_map(
        per_device,
        mesh=mesh,
        in_specs=(
            P("frame", "head", None),
            P(None, "frame", "head", None),
            P("head"),
            P("frame", None),
            P("frame", None),
            P("head", None),
        ),
        out_specs=P(("frame", "head"), None),
        check_vma=False,
    )
```

time: 507 us -> 137 us (0.27); the launches traced: 498 us -> 137 us
  waiting for transfers between devices: 246 us -> 0 us
  Pallas kernels: 0 us -> 135 us
  matrix products: 127 us -> 0 us
  other arithmetic: 58.8 us -> 0 us
  local copies, waits for them, and re-layouts: 42.5 us -> 2.21 us
  between operations: 17.1 us -> 0.01 us
  starting transfers between devices: 5.62 us -> 0 us
    pallas_call x0 -> x1, Pallas kernels: none -> 135 us  [per_device(): pl.pallas_call(kernel, out_shape=jax.ShapeDtypeStruct((ROWS // 8, D), BF1...]
    dot_general x36 -> x0, matrix products: 122 us -> none  [the longest x16 62 us: advance(): lax.dot_general(query_rows, key_rows, (((1,), (1,)), ((), ())), preferred...]
    all_gather x1 -> x0, waiting for transfers between devices: 114 us -> none  [per_device(): lax.all_gather(keys_values, 'frame', axis=1, tiled=True)]
    reduce_scatter x1 -> x0, waiting for transfers between devices: 111 us -> none  [per_device(): lax.psum_scatter(jnp.einsum('htd,hde->te', attention, weight_heads, prefe...]
    reduce_sum x16 -> x0, other arithmetic: 53 us -> none  [advance(): running_sum = running_sum * factor + jnp.sum(exponent, axis=1)]
    ppermute x2 -> x0, waiting for transfers between devices: 21.6 us -> none  [the longest x1 14.6 us: extended(): lax.ppermute(tail, axis, [(i, (i + 1) % count) for i in range(ends)])]
    squeeze x7 -> x0, local copies, waits for them, and re-layouts: 12.8 us -> none  [the longest x2 8.44 us: fold_heads(): shard_piece[1, :, slot_index, :]]
    unnamed x40 -> x1, local copies, waits for them, and re-layouts: 9.72 us -> 2.21 us
  transfers between devices with their start and end apart: 4 -> 0, of which waited for: 4 -> 0; matrix products, arithmetic and copies ran while one was open for 5% -> 0% of each run, Pallas kernels for 0% -> 0%
where the time goes in v1:
time: 137 us
  Pallas kernels  135 us (99%)
  local copies, waits for them, and re-layouts  2.21 us (2%)
    pallas_call x1, Pallas kernels, per_device(): pl.pallas_call(kernel, out_shape=jax.ShapeDtypeStruct((ROWS // 8, D), BF1...  135 us

profile of v1, /device:TPU:8, one launch (start us, length us, event | category | flops | bytes accessed | tf_op | source)
XLA Modules:
  0.0 137.1 jit_solution(687183585769682415)
XLA Ops:
  0.0 134.9 %attend_project.1 = bf16[96,5120]{1,0:T(8,128)(2,1)} custom-call(s32[5]{0:T(128)} %kind_ref.1, s32[2,2]{1,0:T(2,128)} %near_ref.1, s32[2,2]{1,0:T(2,128)} %mask_ref.1, bf16[5,768,128]{2,1,0:T(8,128)(2,1)} %bitcast.3, bf16[2,5,768,128]{3,2,1,0:T(8,128)(2,1)} %bitcast.2, bf16[640,5120]{1,0:T(8,128)(2,1)} %w_hbm.1), custom_call_target="tpu_custom_call" | custom-call | tf_op jit(solution)/shard_map/attend_project/pallas_call | solution.py:479
  134.9 2.2 %copy.8 = bf16[96,5120]{1,0:T(8,128)(2,1)} copy(bf16[96,5120]{1,0:T(8,128)(2,1)} %attend_project.1) | data formatting | bytes 1966080

commit v2 on v1

--- a/solution.py
+++ b/solution.py
@@ -221,7 +221,7 @@
                 bias.append(rows_bias(lambda half: tab[g, s * 2 + half, pl.ds(part * 2 + t, 1), :]))
         return bias
 
-    def temporal(g, b, chunks, first):
+    def temporal(g, b, chunks, first, done=None):
         items = [(s, k) for s in range(2) for k in chunks]
         bias = [temporal_bias(g, s, b) for s in range(2)]
 
@@ -242,24 +242,54 @@
             m, acc = fold(now, kbuf[b, s, 1], bias[s], m, acc)
             m_ref[g, s, rows, :] = m
             acc_ref[g, s, rows, :] = acc
-
-    def send_o(g):
-        for s in range(2):
-            total = acc_ref[g, s, :, HD:]
-            safe = jnp.where(total > 0, total, 1.0)
-            osend[g, s] = (acc_ref[g, s, :, :HD] / safe).astype(BF16)
-            log = m_ref[g, s] + jnp.log2(safe)
-            lsend[g, s] = jnp.transpose(log)[0:8]
-
-    def o_copies(g):
+            if done is not None and k == CH - 1:
+                done(s)
+
+    def o_copies(g, s):
         return (
-            remote(osend.at[g], orecv.at[4 - g], o_ss.at[g], o_rs.at[4 - g], at_y(g)),
-            remote(lsend.at[g], lrecv.at[4 - g], l_ss.at[g], l_rs.at[4 - g], at_y(g)),
+            remote(osend.at[g, s], orecv.at[4 - g, s], o_ss.at[g, s], o_rs.at[4 - g, s], at_y(g)),
+            remote(lsend.at[g, s], lrecv.at[4 - g, s], l_ss.at[g, s], l_rs.at[4 - g, s], at_y(g)),
         )
+
+    def send_o(g, s):
+        total = acc_ref[g, s, :, HD:]
+        safe = jnp.where(total > 0, total, 1.0)
+        osend[g, s] = (acc_ref[g, s, :, :HD] / safe).astype(BF16)
+        log = m_ref[g, s] + jnp.log2(safe)
+        lsend[g, s] = jnp.transpose(log)[0:8]
+        for copy in o_copies(g, s):
+            copy.start()
+
+    def arrived(g):
+        tx[4 - g].wait_recv()
+        qx[4 - g].wait_recv()
+        spread(trecv[g], g)
 
     for s in range(2):
         kc[0][s].wait_recv()
     temporal(0, 0, range(CH), True)
+    arrived(1)
+    temporal(1, 0, range(CH), True)
+    kx[0].wait_recv()
+    start(kc[1][0])
+    arrived(3)
+    temporal(3, 0, range(CH), True)
+    kx[1].wait_recv()
+    start(kc[1][1])
+    for s in range(2):
+        kc[1][s].wait_recv()
+
+    @pl.loop(0, 2)
+    def _(i):
+        g = 1 + 2 * i
+        temporal(g, 1, range(CH), False)
+        for s in range(2):
+            send_o(g, s)
+
+    arrived(2)
+    temporal(2, 0, range(CH), True)
+    temporal(2, 1, range(CH), False, lambda s: send_o(2, s))
+    temporal(0, 1, range(CH), False)
 
     h_next.wait_recv()
     h_prev.wait_recv()
@@ -276,40 +306,6 @@
             ahead = scores(qslide[s1, k1 * CROWS : (k1 + 1) * CROWS, :], wbuf[s1, 0])
         _, acc = fold(now, wbuf[s, 1], window_bias, jnp.full((CROWS, HD), NEG, F32), None)
         attn[k, :, (s + 2) * HD : (s + 3) * HD] = (acc[:, :HD] / acc[:, HD:]).astype(BF16)
-
-    for g in (1, 3):
-        tx[4 - g].wait_recv()
-        qx[4 - g].wait_recv()
-        spread(trecv[g], g)
-
-    kx[0].wait_recv()
-    start(kc[1][0])
-
-    @pl.loop(0, 2)
-    def _(i):
-        temporal(1 + 2 * i, 0, range(CH), True)
-
-    kx[1].wait_recv()
-    start(kc[1][1])
-    for s in range(2):
-        kc[1][s].wait_recv()
-
-    @pl.loop(0, 2)
-    def _(i):
-        g = 1 + 2 * i
-        temporal(g, 1, range(CH), False)
-        send_o(g)
-        for copy in o_copies(g):
-            copy.start()
-
-    tx[2].wait_recv()
-    qx[2].wait_recv()
-    spread(trecv[2], 2)
-    temporal(2, 0, range(CH), True)
-    temporal(2, 1, range(CH), False)
-    send_o(2)
-    for copy in o_copies(2):
-        copy.start()
 
     def combine(k):
         rows = pl.ds(k * CROWS, CROWS)
@@ -442,19 +438,18 @@
             emit(k, H2, HB, xb.at[k, 0, :, pl.ds(HB, HB)], rb.at[k, 0, 1], rb.at[k, 1, 1])
 
     one, two = Chunk(0), Chunk(1)
-    temporal(0, 1, [0], False)
     for g in (1, 3, 2):
-        for copy in o_copies(4 - g):
-            copy.wait_recv()
+        for s in range(2):
+            for copy in o_copies(4 - g, s):
+                copy.wait_recv()
     combine(0)
     load_w.wait()
     project(0)
     one.first()
-    temporal(0, 1, [1], False)
     combine(1)
-    one.forward_a()
     project(1)
     two.first()
+    one.forward_a()
     one.second_b()
     two.forward_a()
     one.third_a()
@@ -468,8 +463,9 @@
     for copy in sent:
         copy.wait_send()
     for g in range(1, 4):
-        for copy in o_copies(g):
-            copy.wait_send()
+        for s in range(2):
+            for copy in o_copies(g, s):
+                copy.wait_send()
 
 
 def per_device(queries, keys_values, head_kind, tile_neighbours, tile_mask, out_weight):
@@ -514,8 +510,8 @@
             dma((2,)), dma((2,)),
             dma((2, 2)), dma((2, 2)),
             dma((2,)), dma((2,)),
-            dma((4,)), dma((4,)),
-            dma((4,)), dma((4,)),
+            dma((4, 2)), dma((4, 2)),
+            dma((4, 2)), dma((4, 2)),
             dma((CH, 20)), dma((CH, 20)),
         ],
         name="attend_project",

time: 137 us -> 122 us (0.89)
  Pallas kernels: 135 us -> 120 us
    pallas_call x1, Pallas kernels: 135 us -> 120 us  [per_device(): pl.pallas_call(kernel, out_shape=jax.ShapeDtypeStruct((ROWS // 8, D), BF1...]
where the time goes in v2:
time: 122 us
  Pallas kernels  120 us (98%)
  local copies, waits for them, and re-layouts  2.21 us (2%)
    pallas_call x1, Pallas kernels, per_device(): pl.pallas_call(kernel, out_shape=jax.ShapeDtypeStruct((ROWS // 8, D), BF1...  120 us

profile of v2, /device:TPU:8, one launch (start us, length us, event | category | flops | bytes accessed | tf_op | source)
XLA Modules:
  0.0 121.9 jit_solution(333582351270197313)
XLA Ops:
  0.0 119.7 %attend_project.1 = bf16[96,5120]{1,0:T(8,128)(2,1)} custom-call(s32[5]{0:T(128)} %kind_ref.1, s32[2,2]{1,0:T(2,128)} %near_ref.1, s32[2,2]{1,0:T(2,128)} %mask_ref.1, bf16[5,768,128]{2,1,0:T(8,128)(2,1)} %bitcast.3, bf16[2,5,768,128]{3,2,1,0:T(8,128)(2,1)} %bitcast.2, bf16[640,5120]{1,0:T(8,128)(2,1)} %w_hbm.1), custom_call_target="tpu_custom_call" | custom-call | tf_op jit(solution)/shard_map/attend_project/pallas_call | solution.py:475
  119.7 2.2 %copy.8 = bf16[96,5120]{1,0:T(8,128)(2,1)} copy(bf16[96,5120]{1,0:T(8,128)(2,1)} %attend_project.1) | data formatting | bytes 1966080

commit v3 on v2

--- a/solution.py
+++ b/solution.py
@@ -177,10 +177,17 @@
     tsend[4:8, :] = jnp.zeros((4, HD), F32)
     window_ids = frame * 2 - 1 + lax.broadcasted_iota(jnp.int32, (8, HD), 0)
     window = [jnp.where(allowed(half, window_ids), 0.0, OFF) for half in range(2)]
-    qx, tx = [None] * 4, [None] * 4
+
+    def query_copy(src, dst, s, g):
+        return remote(qall.at[src, s], qall.at[dst, s], q_ss.at[dst, s], q_rs.at[dst, s], at_y(g))
+
+    up = [start(query_copy(0, 3, 0, 1)), None]
+    down = [None, start(query_copy(0, 1, 1, 3))]
+    up[1] = start(query_copy(0, 3, 1, 1))
+    down[0] = start(query_copy(0, 1, 0, 3))
+    tx = [None] * 4
     for g in (1, 3, 2):
         tx[g] = start(remote(tsend, trecv.at[4 - g], t_ss.at[g], t_rs.at[4 - g], at_y(g)))
-        qx[g] = start(remote(qall.at[0], qall.at[4 - g], q_ss.at[g], q_rs.at[4 - g], at_y(g)))
 
     @pl.loop(0, ROWS // 96)
     def _(r):
@@ -189,11 +196,6 @@
         for s in range(3):
             for t in range(2):
                 wbuf[s, t, to, :] = choose(s + 2, lambda i: kv_ref[t, i, rows, :])
-
-    h_next = start(remote(wbuf.at[:, :, pl.ds(2 * TILE, TILE)], wbuf.at[:, :, pl.ds(0, TILE)],
-                          h_ss.at[0], h_rs.at[0], after))
-    h_prev = start(remote(wbuf.at[:, :, pl.ds(TILE, TILE)], wbuf.at[:, :, pl.ds(3 * TILE, TILE)],
-                          h_ss.at[1], h_rs.at[1], before))
 
     def spread(src, g):
         for i in range(4):
@@ -260,22 +262,30 @@
         for copy in o_copies(g, s):
             copy.start()
 
-    def arrived(g):
-        tx[4 - g].wait_recv()
-        qx[4 - g].wait_recv()
-        spread(trecv[g], g)
-
     for s in range(2):
         kc[0][s].wait_recv()
     temporal(0, 0, range(CH), True)
-    arrived(1)
+    up[0].wait_recv()
+    far = [start(query_copy(3, 2, 0, 1)), None]
+    down[1].wait_recv()
+    far[1] = start(query_copy(1, 2, 1, 3))
+    down[0].wait_recv()
+    up[1].wait_recv()
+    for g in (1, 3, 2):
+        tx[4 - g].wait_recv()
+        spread(trecv[g], g)
+    h_next = start(remote(wbuf.at[:, :, pl.ds(2 * TILE, TILE)], wbuf.at[:, :, pl.ds(0, TILE)],
+                          h_ss.at[0], h_rs.at[0], after))
+    h_prev = start(remote(wbuf.at[:, :, pl.ds(TILE, TILE)], wbuf.at[:, :, pl.ds(3 * TILE, TILE)],
+                          h_ss.at[1], h_rs.at[1], before))
     temporal(1, 0, range(CH), True)
-    kx[0].wait_recv()
-    start(kc[1][0])
-    arrived(3)
     temporal(3, 0, range(CH), True)
-    kx[1].wait_recv()
-    start(kc[1][1])
+    for s in range(2):
+        kx[s].wait_recv()
+        start(kc[1][s])
+    for copy in far:
+        copy.wait_recv()
+    temporal(2, 0, range(CH), True)
     for s in range(2):
         kc[1][s].wait_recv()
 
@@ -286,8 +296,6 @@
         for s in range(2):
             send_o(g, s)
 
-    arrived(2)
-    temporal(2, 0, range(CH), True)
     temporal(2, 1, range(CH), False, lambda s: send_o(2, s))
     temporal(0, 1, range(CH), False)
 
@@ -324,9 +332,9 @@
                 mixed / functools.reduce(jnp.add, weights)
             ).astype(BF16)
 
-    WIDTH = 512
-
-    def project(k):
+    WIDTH = 768
+
+    def reorder(k):
         slots = [attn[k, :, s * HD : (s + 1) * HD] for s in range(5)]
         for i in range(5):
             value = slots[0]
@@ -335,10 +343,17 @@
                     value = lax.select(order[s] == i, slots[s], value)
             attn[k, :, i * HD : (i + 1) * HD] = value
 
-        @pl.loop(0, D // WIDTH)
+    def project(k, first, last):
+        whole = (last - first) // WIDTH
+
+        @pl.loop(0, whole)
         def _(j):
-            columns = pl.ds(pl.multiple_of(j * WIDTH, WIDTH), WIDTH)
+            columns = pl.ds(pl.multiple_of(first + j * WIDTH, 128), WIDTH)
             pbuf[k, :, columns] = dot(attn[k], w_ref[:, columns], 1, 0).astype(BF16)
+
+        rest = first + whole * WIDTH
+        if rest < last:
+            pbuf[k, :, rest:last] = dot(attn[k], w_ref[:, rest:last], 1, 0).astype(BF16)
 
     def block(k, zr, xr, first, width):
         return pbuf.at[k, pl.ds((zr * 2 + xr) * DROWS, DROWS), pl.ds(first, width)]
@@ -373,19 +388,22 @@
             self.count += 1
             return start(remote(src, dst, r_ss.at[self.k, n], r_rs.at[self.k, n], peer))
 
-        def first(self):
+        def first_a(self):
             k = self.k
             self.fa = [
                 self.send(block(k, 2, 0, 0, CA), fa.at[k, 0], z_up),
                 self.send(block(k, 2, 1, 0, CA), fa.at[k, 1], z_down),
             ]
-            self.xb = {}
-            for zr in (2, 1, 3, 0):
-                self.xb[zr] = self.send(block(k, zr, 1, CA, CB), xb.at[k, zr], x_other)
             self.ra = [
                 self.send(block(k, 1, 1, 0, CA), ra.at[k, 0, 1], z_up),
                 self.send(block(k, 3, 0, 0, CA), ra.at[k, 1, 0], z_down),
             ]
+
+        def first_b(self):
+            k = self.k
+            self.xb = {}
+            for zr in (2, 1, 3, 0):
+                self.xb[zr] = self.send(block(k, zr, 1, CA, CB), xb.at[k, zr], x_other)
 
         def forward_a(self):
             k = self.k
@@ -443,13 +461,19 @@
             for copy in o_copies(4 - g, s):
                 copy.wait_recv()
     combine(0)
+    reorder(0)
     load_w.wait()
-    project(0)
-    one.first()
+    project(0, CA, D)
+    one.first_b()
+    project(0, 0, CA)
+    one.first_a()
     combine(1)
-    project(1)
-    two.first()
+    reorder(1)
+    project(1, CA, D)
+    two.first_b()
     one.forward_a()
+    project(1, 0, CA)
+    two.first_a()
     one.second_b()
     two.forward_a()
     one.third_a()
@@ -505,7 +529,7 @@
             pltpu.VMEM((CH, 2, DROWS, HB), BF16),
             pltpu.VMEM((CH, 2, 2, DROWS, HB), BF16),
             dma,
-            dma((4,)), dma((4,)),
+            dma((4, 2)), dma((4, 2)),
             dma((4,)), dma((4,)),
             dma((2,)), dma((2,)),
             dma((2, 2)), dma((2, 2)),

time: 122 us -> 118 us (0.967)
  Pallas kernels: 120 us -> 115 us
    pallas_call x1, Pallas kernels: 120 us -> 115 us  [per_device(): pl.pallas_call(kernel, out_shape=jax.ShapeDtypeStruct((ROWS // 8, D), BF1...]
where the time goes in v3:
time: 118 us
  Pallas kernels  115 us (97%)
  local copies, waits for them, and re-layouts  2.21 us (2%)
    pallas_call x1, Pallas kernels, per_device(): pl.pallas_call(kernel, out_shape=jax.ShapeDtypeStruct((ROWS // 8, D), BF1...  115 us

profile of v3, /device:TPU:8, one launch (start us, length us, event | category | flops | bytes accessed | tf_op | source)
XLA Modules:
  0.0 117.7 jit_solution(3549969759674670516)
XLA Ops:
  0.0 115.5 %attend_project.1 = bf16[96,5120]{1,0:T(8,128)(2,1)} custom-call(s32[5]{0:T(128)} %kind_ref.1, s32[2,2]{1,0:T(2,128)} %near_ref.1, s32[2,2]{1,0:T(2,128)} %mask_ref.1, bf16[5,768,128]{2,1,0:T(8,128)(2,1)} %bitcast.3, bf16[2,5,768,128]{3,2,1,0:T(8,128)(2,1)} %bitcast.2, bf16[640,5120]{1,0:T(8,128)(2,1)} %w_hbm.1), custom_call_target="tpu_custom_call" | custom-call | tf_op jit(solution)/shard_map/attend_project/pallas_call | solution.py:499
  115.5 2.2 %copy.8 = bf16[96,5120]{1,0:T(8,128)(2,1)} copy(bf16[96,5120]{1,0:T(8,128)(2,1)} %attend_project.1) | data formatting | bytes 1966080

commit v4 on v3

--- a/solution.py
+++ b/solution.py
@@ -20,9 +20,12 @@
 CROWS = ROWS // CH
 DROWS = CROWS // 8
 ZROWS = 2 * DROWS
-CA = 2816
-CB = D - CA
-HB = CB // 2
+CA = 1536
+CB = 1536
+CE = D - CA - CB
+EW = CA + CB
+HB, HE = CB // 2, CE // 2
+WROWS = 5 * HD // 2
 NEG = -1e30
 OFF = -2e30
 SCALE = HD**-0.5 * math.log2(math.e)
@@ -64,9 +67,9 @@
     kind_ref, near_ref, mask_ref, q_ref, kv_ref, w_hbm, out_ref,
     w_ref, qall, qslide, kbuf, wbuf, tsend, trecv, tab, m_ref, acc_ref,
     osend, lsend, orecv, lrecv, attn, pbuf,
-    fa, ra, xa, xb, fb, rb,
+    fa, ra, xa, xb, fb, rb, wx, asend, arecv, fe, re,
     w_sem, q_ss, q_rs, t_ss, t_rs, kx_ss, kx_rs, kc_ss, kc_rs, h_ss, h_rs,
-    o_ss, o_rs, l_ss, l_rs, r_ss, r_rs,
+    o_ss, o_rs, l_ss, l_rs, r_ss, r_rs, wx_ss, wx_rs, a_ss, a_rs,
 ):
     frame = lax.axis_index("frame")
     head = lax.axis_index("head")
@@ -283,6 +286,10 @@
     for s in range(2):
         kx[s].wait_recv()
         start(kc[1][s])
+    load_w.wait()
+    mine = pl.ds(pl.multiple_of(c * WROWS, 16), WROWS)
+    w_cross = start(remote(w_ref.at[mine, pl.ds(EW, CE)], wx.at[mine], wx_ss.at[0], wx_rs.at[0], x_other))
+    w_core = remote(wx.at[mine], wx.at[mine], wx_ss.at[1], wx_rs.at[1], core)
     for copy in far:
         copy.wait_recv()
     temporal(2, 0, range(CH), True)
@@ -355,6 +362,26 @@
         if rest < last:
             pbuf[k, :, rest:last] = dot(attn[k], w_ref[:, rest:last], 1, 0).astype(BF16)
 
+    def exchange(k):
+        for zr in range(4):
+            at = (zr * 2 + 1) * DROWS
+            asend[k, zr * DROWS : (zr + 1) * DROWS, :] = attn[k, at : at + DROWS, :]
+        return start(remote(asend.at[k], arecv.at[k], a_ss.at[k], a_rs.at[k], x_other))
+
+    def project_two(k):
+        kept = jnp.concatenate(
+            [attn[k, zr * ZROWS : zr * ZROWS + DROWS, :] for zr in range(4)], axis=0
+        )
+
+        @pl.loop(0, CE // 512)
+        def _(j):
+            columns = pl.ds(pl.multiple_of(EW + j * 512, 512), 512)
+            others = pl.ds(pl.multiple_of(j * 512, 512), 512)
+            value = dot(kept, w_ref[:, columns], 1, 0) + dot(arecv[k], wx[:, others], 1, 0)
+            value = value.astype(BF16)
+            for zr in range(4):
+                pbuf[k, zr * ZROWS : zr * ZROWS + DROWS, columns] = value[zr * DROWS : (zr + 1) * DROWS]
+
     def block(k, zr, xr, first, width):
         return pbuf.at[k, pl.ds((zr * 2 + xr) * DROWS, DROWS), pl.ds(first, width)]
 
@@ -429,6 +456,33 @@
             add(k, 3, 0, CA, CB, xb.at[k, 3])
             self.rb.append(self.send(block(k, 3, 0, H1, HB), rb.at[k, 1, 0], z_down))
 
+        def first_e(self):
+            k = self.k
+            self.fe = [
+                self.send(block(k, 2, 0, EW, HE), fe.at[k, 0], z_up),
+                self.send(block(k, 2, 0, EW + HE, HE), fe.at[k, 1], z_down),
+            ]
+            self.re = [
+                self.send(block(k, 1, 0, EW + HE, HE), re.at[k, 0, 1], z_up),
+                self.send(block(k, 3, 0, EW, HE), re.at[k, 1, 0], z_down),
+            ]
+
+        def forward_e(self):
+            k = self.k
+            self.fe[0].wait_recv()
+            add(k, 1, 0, EW, HE, fe.at[k, 0])
+            self.re.append(self.send(block(k, 1, 0, EW, HE), re.at[k, 0, 0], z_up))
+            self.fe[1].wait_recv()
+            add(k, 3, 0, EW + HE, HE, fe.at[k, 1])
+            self.re.append(self.send(block(k, 3, 0, EW + HE, HE), re.at[k, 1, 1], z_down))
+
+        def finish_e(self):
+            k = self.k
+            for copy in self.re:
+                copy.wait_recv()
+            emit(k, EW, HE, re.at[k, 0, 0], re.at[k, 1, 0])
+            emit(k, EW + HE, HE, re.at[k, 0, 1], re.at[k, 1, 1])
+
         def third_a(self):
             k = self.k
             for copy in self.ra:
@@ -462,25 +516,39 @@
                 copy.wait_recv()
     combine(0)
     reorder(0)
-    load_w.wait()
-    project(0, CA, D)
+    crossed = [exchange(0)]
+    project(0, CA, EW)
     one.first_b()
     project(0, 0, CA)
     one.first_a()
+    w_cross.wait_recv()
+    start(w_core)
     combine(1)
     reorder(1)
-    project(1, CA, D)
+    crossed.append(exchange(1))
+    project(1, CA, EW)
     two.first_b()
-    one.forward_a()
     project(1, 0, CA)
     two.first_a()
+    w_core.wait_recv()
+    crossed[0].wait_recv()
+    project_two(0)
+    one.first_e()
+    one.forward_a()
+    crossed[1].wait_recv()
+    project_two(1)
+    two.first_e()
+    two.forward_a()
+    one.forward_e()
     one.second_b()
-    two.forward_a()
     one.third_a()
+    two.forward_e()
     one.forward_b()
     two.second_b()
     two.third_a()
     two.forward_b()
+    one.finish_e()
+    two.finish_e()
     one.finish()
     two.finish()
 
@@ -528,6 +596,11 @@
             pltpu.VMEM((CH, 4, DROWS, CB), BF16),
             pltpu.VMEM((CH, 2, DROWS, HB), BF16),
             pltpu.VMEM((CH, 2, 2, DROWS, HB), BF16),
+            pltpu.VMEM((5 * HD, CE), BF16),
+            pltpu.VMEM((CH, CROWS // 2, 5 * HD), BF16),
+            pltpu.VMEM((CH, CROWS // 2, 5 * HD), BF16),
+            pltpu.VMEM((CH, 2, DROWS, HE), BF16),
+            pltpu.VMEM((CH, 2, 2, DROWS, HE), BF16),
             dma,
             dma((4, 2)), dma((4, 2)),
             dma((4,)), dma((4,)),
@@ -536,7 +609,9 @@
             dma((2,)), dma((2,)),
             dma((4, 2)), dma((4, 2)),
             dma((4, 2)), dma((4, 2)),
-            dma((CH, 20)), dma((CH, 20)),
+            dma((CH, 30)), dma((CH, 30)),
+            dma((2,)), dma((2,)),
+            dma((CH,)), dma((CH,)),
         ],
         name="attend_project",
         compiler_params=pltpu.CompilerParams(

time: 118 us -> 116 us (0.983)
  the two profiles are of different devices: /device:TPU:8 before, /device:TPU:24 now
where the time goes in v4:
time: 116 us
  Pallas kernels  114 us (98%)
  local copies, waits for them, and re-layouts  2.21 us (2%)
    pallas_call x1, Pallas kernels, per_device(): pl.pallas_call(kernel, out_shape=jax.ShapeDtypeStruct((ROWS // 8, D), BF1...  114 us

profile of v4, /device:TPU:24, one launch (start us, length us, event | category | flops | bytes accessed | tf_op | source)
XLA Modules:
  0.0 115.8 jit_solution(6967909129913239405)
XLA Ops:
  0.0 113.6 %attend_project.1 = bf16[96,5120]{1,0:T(8,128)(2,1)} custom-call(s32[5]{0:T(128)} %kind_ref.1, s32[2,2]{1,0:T(2,128)} %near_ref.1, s32[2,2]{1,0:T(2,128)} %mask_ref.1, bf16[5,768,128]{2,1,0:T(8,128)(2,1)} %bitcast.3, bf16[2,5,768,128]{3,2,1,0:T(8,128)(2,1)} %bitcast.2, bf16[640,5120]{1,0:T(8,128)(2,1)} %w_hbm.1), custom_call_target="tpu_custom_call" | custom-call | tf_op jit(solution)/shard_map/attend_project/pallas_call | solution.py:567
  113.6 2.2 %copy.8 = bf16[96,5120]{1,0:T(8,128)(2,1)} copy(bf16[96,5120]{1,0:T(8,128)(2,1)} %attend_project.1) | data formatting | bytes 1966080

commit v5 on v4

--- a/solution.py
+++ b/solution.py
@@ -20,8 +20,8 @@
 CROWS = ROWS // CH
 DROWS = CROWS // 8
 ZROWS = 2 * DROWS
-CA = 1536
-CB = 1536
+CA = 2048
+CB = 1024
 CE = D - CA - CB
 EW = CA + CB
 HB, HE = CB // 2, CE // 2

time: 116 us -> 114 us (0.983)
  the two profiles are of different devices: /device:TPU:24 before, /device:TPU:8 now
where the time goes in v5:
time: 114 us; the launch traced here: 113 us
  Pallas kernels  111 us (97%)
  local copies, waits for them, and re-layouts  2.21 us (2%)
    pallas_call x1, Pallas kernels, per_device(): pl.pallas_call(kernel, out_shape=jax.ShapeDtypeStruct((ROWS // 8, D), BF1...  111 us

profile of v5, /device:TPU:8, one launch (start us, length us, event | category | flops | bytes accessed | tf_op | source)
XLA Modules:
  0.0 113.2 jit_solution(5894537488267627619)
XLA Ops:
  0.0 111.0 %attend_project.1 = bf16[96,5120]{1,0:T(8,128)(2,1)} custom-call(s32[5]{0:T(128)} %kind_ref.1, s32[2,2]{1,0:T(2,128)} %near_ref.1, s32[2,2]{1,0:T(2,128)} %mask_ref.1, bf16[5,768,128]{2,1,0:T(8,128)(2,1)} %bitcast.3, bf16[2,5,768,128]{3,2,1,0:T(8,128)(2,1)} %bitcast.2, bf16[640,5120]{1,0:T(8,128)(2,1)} %w_hbm.1), custom_call_target="tpu_custom_call" | custom-call | tf_op jit(solution)/shard_map/attend_project/pallas_call | solution.py:567
  111.0 2.2 %copy.8 = bf16[96,5120]{1,0:T(8,128)(2,1)} copy(bf16[96,5120]{1,0:T(8,128)(2,1)} %attend_project.1) | data formatting | bytes 1966080

commit v6 on v5

--- a/solution.py
+++ b/solution.py
@@ -526,6 +526,7 @@
     combine(1)
     reorder(1)
     crossed.append(exchange(1))
+    one.forward_a()
     project(1, CA, EW)
     two.first_b()
     project(1, 0, CA)
@@ -534,11 +535,10 @@
     crossed[0].wait_recv()
     project_two(0)
     one.first_e()
-    one.forward_a()
+    two.forward_a()
     crossed[1].wait_recv()
     project_two(1)
     two.first_e()
-    two.forward_a()
     one.forward_e()
     one.second_b()
     one.third_a()

time: 114 us -> 113 us (level)
  no operation moved by 1% of the time
where the time goes in v6:
time: 113 us
  Pallas kernels  111 us (98%)
  local copies, waits for them, and re-layouts  2.21 us (2%)
    pallas_call x1, Pallas kernels, per_device(): pl.pallas_call(kernel, out_shape=jax.ShapeDtypeStruct((ROWS // 8, D), BF1...  111 us

profile of v6, /device:TPU:8, one launch (start us, length us, event | category | flops | bytes accessed | tf_op | source)
XLA Modules:
  0.0 113.2 jit_solution(5534238576304432466)
XLA Ops:
  0.0 111.0 %attend_project.1 = bf16[96,5120]{1,0:T(8,128)(2,1)} custom-call(s32[5]{0:T(128)} %kind_ref.1, s32[2,2]{1,0:T(2,128)} %near_ref.1, s32[2,2]{1,0:T(2,128)} %mask_ref.1, bf16[5,768,128]{2,1,0:T(8,128)(2,1)} %bitcast.3, bf16[2,5,768,128]{3,2,1,0:T(8,128)(2,1)} %bitcast.2, bf16[640,5120]{1,0:T(8,128)(2,1)} %w_hbm.1), custom_call_target="tpu_custom_call" | custom-call | tf_op jit(solution)/shard_map/attend_project/pallas_call | solution.py:567
  111.0 2.2 %copy.8 = bf16[96,5120]{1,0:T(8,128)(2,1)} copy(bf16[96,5120]{1,0:T(8,128)(2,1)} %attend_project.1) | data formatting | bytes 1966080
